TPU v7x, 256 devices: a whole 4x4x8 slice. The times are simulated.
256 devices in a mesh: dp: 64 (over z, y, x_hi), sy: 2 (over x_lo), sx: 2 (over core).
Axes of the slice: x: 4 (x_hi: 2, x_lo: 2; x = x_hi * 2 + x_lo), y: 4, z: 8, core: 2. Of those that a mesh axis runs over, the one named last changes fastest.
Arguments:
- features: bfloat16 [64, 56, 56, 256], P('dp', 'sy', 'sx'), may hold values from -8 to 8
- labels: int32 [64], P('dp'), may hold values from 0 to 999
- grid: int32 [2], replicated, may hold values from 0 to 49
- w_reduce: bfloat16 [3, 256, 64], P(None, None, 'dp'), may hold values from -0.375 to 0.375
- w_spatial: bfloat16 [3, 3, 3, 64, 64], P(None, None, None, None, 'dp'), may hold values from -0.25 to 0.25
- w_expand: bfloat16 [3, 64, 256], P(None, None, 'dp'), may hold values from -0.75 to 0.75
- w_class: bfloat16 [256, 1000], P('dp'), may hold values from -1.5 to 1.5
- dir_reduce: bfloat16 [2, 3, 256, 64], P(None, None, None, 'dp'), may hold values from -6 to 6
- dir_spatial: bfloat16 [2, 3, 3, 3, 64, 64], P(None, None, None, None, None, 'dp'), may hold values from -6 to 6
- dir_expand: bfloat16 [2, 3, 64, 256], P(None, None, None, 'dp'), may hold values from -6 to 6
- dir_class: bfloat16 [2, 256, 1000], P(None, 'dp'), may hold values from -6 to 6
- gain_mid: float32 [3, 2, 64], replicated, may hold values from 0.5 to 1.5
- shift_mid: float32 [3, 2, 64], replicated, may hold values from -3 to 3
- gain_out: float32 [3, 256], replicated, may hold values from 0.5 to 1.5
- shift_out: float32 [3, 256], replicated, may hold values from -3 to 3
Outputs:
- section_out: bfloat16 [64, 56, 56, 256], P('dp', 'sy', 'sx')
- image_loss: float32 [64], P('dp')
- mean_loss: float32 [], replicated
All inputs are finite; a program needn't handle non-finite values.
Results may differ from a plain program's by a relative error of at most 0.012.
Values may be sent and summed in bfloat16 or wider, within the bound.
No kernel may reach another device: no remote copies, remote signals or barrier semaphores. Data moves between devices by JAX's collectives and lax.ppermute only.
A program may use at most 64 MiB of HBM per device.

v0:
```python
import functools

import jax
import jax.numpy as jnp
from jax import lax
from jax.sharding import Mesh
from jax.sharding import PartitionSpec as P

BLOCKS = 3
GRID = 50
DP = ("dp_0", "dp_1", "dp_2")
DP_SY_SX = ("dp_0", "dp_1", "dp_2", "sy", "sx")


EPS_NORM = 1e-06
EPS_BN = 1e-05


def in_order(blocks, dim):
    lengths = list(blocks.shape[1:])
    lengths[dim] *= blocks.shape[0]
    return jnp.moveaxis(blocks, 0, dim).reshape(lengths)


def copy_for_each(value, axis):
    length = lax.axis_size(axis)
    return lax.all_to_all(
        jnp.broadcast_to(value[None], (length, *value.shape)), axis, 0, 0, tiled=True
    )


def gathered_copies(value, axis, dim):
    return in_order(copy_for_each(value, axis), dim)


def one_axis_at_a_time(value, axes):
    return functools.reduce(lax.psum, axes, value)


def extended(cells, sides, width):
    for axis, dim in sides:
        count = lax.axis_size(axis)
        ends = count - 1
        head = lax.slice_in_dim(cells, 0, width, axis=dim)
        tail = lax.slice_in_dim(cells, cells.shape[dim] - width, cells.shape[dim], axis=dim)
        cells = jnp.concatenate(
            [
                lax.ppermute(tail, axis, [(i, (i + 1) % count) for i in range(ends)]),
                cells,
                lax.ppermute(head, axis, [((i + 1) % count, i) for i in range(ends)]),
            ],
            axis=dim,
        )
    return cells


def over_copies(value, axis):
    everything = copy_for_each(value, axis)
    return jnp.sum(everything, axis=0)


def in_one(arrays, axis):
    ends = [0]
    for a in arrays:
        ends.append(ends[-1] + a.size)
    subtotal = over_copies(jnp.concatenate([a.ravel() for a in arrays]), axis)
    return tuple((subtotal[b:e].reshape(a.shape) for a, b, e in zip(arrays, ends, ends[1:])))


def coefficients(grid):
    values = grid.astype(jnp.float32)
    alpha = (2.0 * values + 1.0 - GRID) / GRID
    return (alpha[0], alpha[1])


def filter_ratio(base, direction):
    base_norm = jnp.sqrt(jnp.sum(jnp.square(base.astype(jnp.float32)), axis=0, keepdims=True))
    dir_norm = jnp.sqrt(
        jnp.sum(jnp.square(direction.astype(jnp.float32)), axis=0, keepdims=True) + EPS_NORM
    )
    return base_norm / dir_norm


def combine_filters(base, dir_a, dir_b, alpha_a, alpha_b):
    ratio_a = filter_ratio(base, dir_a)
    ratio_b = filter_ratio(base, dir_b)
    value = (
        base.astype(jnp.float32)
        + alpha_a * ratio_a * dir_a.astype(jnp.float32)
        + alpha_b * ratio_b * dir_b.astype(jnp.float32)
    )
    return value.astype(jnp.bfloat16)


def perturbed_product(left, base, dir_a, dir_b, alpha_a, alpha_b):
    local = combine_filters(base, dir_a, dir_b, alpha_a, alpha_b)
    return jnp.dot(left, gathered_copies(local, DP, 1), preferred_element_type=jnp.float32)


def normalize(y, gain, shift, count):
    total, squares = (
        one_axis_at_a_time(jnp.sum(y, axis=0), DP_SY_SX),
        one_axis_at_a_time(jnp.sum(y * y, axis=0), DP_SY_SX),
    )
    mean = total / count
    var = jnp.maximum(squares / count - mean * mean, 0.0)
    centred = y - mean
    return centred * lax.rsqrt(var + EPS_BN) * gain + shift


def padded_tile(inner):
    return extended(inner, (("sy", 1), ("sx", 2)), 1)


def per_device(
    features,
    labels,
    grid,
    w_reduce,
    w_spatial,
    w_expand,
    w_class,
    dir_reduce,
    dir_spatial,
    dir_expand,
    dir_class,
    gain_mid,
    shift_mid,
    gain_out,
    shift_out,
):
    alpha_a, alpha_b = coefficients(grid)
    images, rows, cols, width = features.shape
    tiles = lax.axis_size("sy") * lax.axis_size("sx")
    count = images * rows * cols * lax.axis_size(DP) * tiles
    inner_width = w_spatial.shape[3]
    current = features
    for block in range(BLOCKS):
        flat = current.reshape(-1, width)
        first = perturbed_product(
            flat, w_reduce[block], dir_reduce[0, block], dir_reduce[1, block], alpha_a, alpha_b
        )
        first = jax.nn.relu(
            normalize(first, gain_mid[block, 0], shift_mid[block, 0], count)
        ).astype(jnp.bfloat16)
        framed = padded_tile(first.reshape(images, rows, cols, inner_width))
        patches = jnp.concatenate(
            [framed[:, i : i + rows, j : j + cols, :] for i in range(3) for j in range(3)], axis=-1
        )
        patches = patches.reshape(-1, 9 * inner_width)
        spatial_base = w_spatial[block].reshape(9 * inner_width, -1)
        spatial_a = dir_spatial[0, block].reshape(9 * inner_width, -1)
        spatial_b = dir_spatial[1, block].reshape(9 * inner_width, -1)
        second = perturbed_product(patches, spatial_base, spatial_a, spatial_b, alpha_a, alpha_b)
        second = jax.nn.relu(
            normalize(second, gain_mid[block, 1], shift_mid[block, 1], count)
        ).astype(jnp.bfloat16)
        third = perturbed_product(
            second, w_expand[block], dir_expand[0, block], dir_expand[1, block], alpha_a, alpha_b
        )
        third = normalize(third, gain_out[block], shift_out[block], count)
        current = (
            jax.nn.relu(flat.astype(jnp.float32) + third)
            .astype(jnp.bfloat16)
            .reshape(images, rows, cols, width)
        )
    pooled_part = jnp.sum(current.astype(jnp.float32), axis=(1, 2))
    pooled = (over_copies(pooled_part, ("sy", "sx")) / (rows * cols * tiles)).astype(jnp.bfloat16)
    class_a = dir_class[0]
    class_b = dir_class[1]
    norm_base, norm_a, norm_b = in_one(
        (
            jnp.sum(jnp.square(w_class.astype(jnp.float32)), axis=0),
            jnp.sum(jnp.square(class_a.astype(jnp.float32)), axis=0),
            jnp.sum(jnp.square(class_b.astype(jnp.float32)), axis=0),
        ),
        DP,
    )
    ratio_a = jnp.sqrt(norm_base) / jnp.sqrt(norm_a + EPS_NORM)
    ratio_b = jnp.sqrt(norm_base) / jnp.sqrt(norm_b + EPS_NORM)
    local_class = (
        w_class.astype(jnp.float32)
        + alpha_a * ratio_a * class_a.astype(jnp.float32)
        + alpha_b * ratio_b * class_b.astype(jnp.float32)
    ).astype(jnp.bfloat16)
    logits = jnp.dot(
        pooled, gathered_copies(local_class, DP, 0), preferred_element_type=jnp.float32
    )
    summed = jnp.log(jnp.sum(jnp.exp(logits), axis=1))
    classes = lax.broadcasted_iota(jnp.int32, logits.shape, 1)
    picked = jnp.sum(jnp.where(classes == labels[:, None], logits, 0.0), axis=1)
    image_loss = summed - picked
    mean_loss = over_copies(jnp.sum(image_loss), DP) / (images * lax.axis_size(DP))
    return (current, image_loss, mean_loss)


def solution(mesh):
    split = Mesh(
        mesh.devices.reshape(8, 4, 2, mesh.shape["sy"], mesh.shape["sx"]),
        ("dp_0", "dp_1", "dp_2", "sy", "sx"),
    )
    return jax.shard_map(
        per_device,
        mesh=split,
        in_specs=(
            P(DP, "sy", "sx", None),
            P(DP),
            P(),
            P(None, None, DP),
            P(None, None, None, None, DP),
            P(None, None, DP),
            P(DP, None),
            P(None, None, None, DP),
            P(None, None, None, None, None, DP),
            P(None, None, None, DP),
            P(None, DP, None),
            P(),
            P(),
            P(),
            P(),
        ),
        out_specs=(P(DP, "sy", "sx", None), P(DP), P()),
        check_vma=False,
    )
```

profile of v0, /device:TPU:1, one launch (start us, length us, event | category | flops | bytes accessed | tf_op | source)
XLA Modules:
  0.0 652.8 jit_solution(7499623723333664865)
XLA Ops:
  16.7 15.2 %all-to-all-start = ((bf16[64,2,128]{2,1,0:T(2,128)(2,1)}), bf16[64,2,128]{2,1,0:T(2,128)(2,1)S(1)}, u32[]{:S(2)}, u32[]{:S(2)}) async-start(bf16[64,2,128]{2,1,0:T(2,128)(2,1)} %reshape.1069), calls=%async_computation | async-start | bytes 65536 | tf_op jit(solution)/shard_map/all_to_all | solution.py:27
  50.1 12.1 %all-to-all-start.2 = ((bf16[64,2,128]{2,1,0:T(2,128)(2,1)}), bf16[64,2,128]{2,1,0:T(2,128)(2,1)S(1)}, u32[]{:S(2)}, u32[]{:S(2)}) async-start(bf16[64,2,128]{2,1,0:T(2,128)(2,1)} %reshape.1067), calls=%async_computation.2 | async-start | bytes 65536 | tf_op jit(solution)/shard_map/all_to_all | solution.py:27
  62.7 14.1 %all-reduce.8 = (f32[64]{0:T(128)S(1)}, f32[64]{0:T(128)S(1)}) all-reduce(f32[64]{0:T(128)S(1)} %get-tuple-element.20, f32[64]{0:T(128)S(1)} %get-tuple-element.19), channel_id=1, replica_groups=mesh['dp_0'=8,'dp_1'=4,'dp_2'=2,'sy'=2,'sx'=2] {'dp_0'}, use_global_device_ids=true, to_apply=%region_10.0 | all-reduce | flops 128 | bytes 1024 | tf_op jit(solution)/shard_map/psum | solution.py:37
  76.7 8.4 %all-reduce.17 = (f32[64]{0:T(128)S(1)}, f32[64]{0:T(128)S(1)}) all-reduce(f32[64]{0:T(128)S(1)} %get-tuple-element.77, f32[64]{0:T(128)S(1)} %get-tuple-element.78), channel_id=1, replica_groups=mesh['dp_0'=8,'dp_1'=4,'dp_2'=2,'sy'=2,'sx'=2] {'dp_1'}, use_global_device_ids=true, to_apply=%region_11.0 | all-reduce | flops 128 | bytes 1024 | tf_op jit(solution)/shard_map/psum | solution.py:37
  94.2 11.1 %all-reduce.26 = (f32[64]{0:T(128)S(1)}, f32[64]{0:T(128)S(1)}) all-reduce(f32[64]{0:T(128)S(1)} %get-tuple-element.131, f32[64]{0:T(128)S(1)} %get-tuple-element.132), channel_id=1, replica_groups=mesh['dp_0'=8,'dp_1'=4,'dp_2'=2,'sy'=2,'sx'=2] {'sx'}, use_global_device_ids=true, to_apply=%region_14.0 | all-reduce | flops 128 | bytes 1024 | tf_op jit(solution)/shard_map/psum | solution.py:37
  120.1 8.5 %all-to-all-start.3 = ((bf16[64,2,128]{2,1,0:T(2,128)(2,1)}), bf16[64,2,128]{2,1,0:T(2,128)(2,1)S(1)}, u32[]{:S(2)}, u32[]{:S(2)}) async-start(bf16[64,2,128]{2,1,0:T(2,128)(2,1)} %reshape.1073), calls=%async_computation.3 | async-start | bytes 65536 | tf_op jit(solution)/shard_map/all_to_all | solution.py:27
  163.7 13.7 %all-reduce.7 = (f32[64]{0:T(128)S(1)}, f32[64]{0:T(128)S(1)}) all-reduce(f32[64]{0:T(128)S(1)} %get-tuple-element.18, f32[64]{0:T(128)S(1)} %get-tuple-element.17), channel_id=1, replica_groups=mesh['dp_0'=8,'dp_1'=4,'dp_2'=2,'sy'=2,'sx'=2] {'dp_0'}, use_global_device_ids=true, to_apply=%region_25.26 | all-reduce | flops 128 | bytes 1024 | tf_op jit(solution)/shard_map/psum | solution.py:37
  177.4 8.4 %all-reduce.16 = (f32[64]{0:T(128)S(1)}, f32[64]{0:T(128)S(1)}) all-reduce(f32[64]{0:T(128)S(1)} %get-tuple-element.75, f32[64]{0:T(128)S(1)} %get-tuple-element.76), channel_id=1, replica_groups=mesh['dp_0'=8,'dp_1'=4,'dp_2'=2,'sy'=2,'sx'=2] {'dp_1'}, use_global_device_ids=true, to_apply=%region_26.27 | all-reduce | flops 128 | bytes 1024 | tf_op jit(solution)/shard_map/psum | solution.py:37
  194.9 11.6 %all-reduce.25 = (f32[64]{0:T(128)S(1)}, f32[64]{0:T(128)S(1)}) all-reduce(f32[64]{0:T(128)S(1)} %get-tuple-element.129, f32[64]{0:T(128)S(1)} %get-tuple-element.130), channel_id=1, replica_groups=mesh['dp_0'=8,'dp_1'=4,'dp_2'=2,'sy'=2,'sx'=2] {'sx'}, use_global_device_ids=true, to_apply=%region_29.30 | all-reduce | flops 128 | bytes 1024 | tf_op jit(solution)/shard_map/psum | solution.py:37
  207.7 11.6 %all-reduce.6 = (f32[256]{0:T(256)S(1)}, f32[256]{0:T(256)S(1)}) all-reduce(f32[256]{0:T(256)S(1)} %get-tuple-element.8, f32[256]{0:T(256)S(1)} %get-tuple-element.7), channel_id=1, replica_groups=mesh['dp_0'=8,'dp_1'=4,'dp_2'=2,'sy'=2,'sx'=2] {'dp_0'}, use_global_device_ids=true, to_apply=%region_40.41 | all-reduce | flops 512 | bytes 4096 | tf_op jit(solution)/shard_map/psum | solution.py:37
  234.3 10.0 %all-reduce.24 = (f32[256]{0:T(256)S(1)}, f32[256]{0:T(256)S(1)}) all-reduce(f32[256]{0:T(256)S(1)} %get-tuple-element.127, f32[256]{0:T(256)S(1)} %get-tuple-element.128), channel_id=1, replica_groups=mesh['dp_0'=8,'dp_1'=4,'dp_2'=2,'sy'=2,'sx'=2] {'sx'}, use_global_device_ids=true, to_apply=%region_44.45 | all-reduce | flops 512 | bytes 4096 | tf_op jit(solution)/shard_map/psum | solution.py:37
  246.2 11.6 %all-reduce.5 = (f32[64]{0:T(128)S(1)}, f32[64]{0:T(128)S(1)}) all-reduce(f32[64]{0:T(128)S(1)} %get-tuple-element.16, f32[64]{0:T(128)S(1)} %get-tuple-element.15), channel_id=1, replica_groups=mesh['dp_0'=8,'dp_1'=4,'dp_2'=2,'sy'=2,'sx'=2] {'dp_0'}, use_global_device_ids=true, to_apply=%region_55.56 | all-reduce | flops 128 | bytes 1024 | tf_op jit(solution)/shard_map/psum | solution.py:37
  257.9 7.7 %all-reduce.14 = (f32[64]{0:T(128)S(1)}, f32[64]{0:T(128)S(1)}) all-reduce(f32[64]{0:T(128)S(1)} %get-tuple-element.71, f32[64]{0:T(128)S(1)} %get-tuple-element.72), channel_id=1, replica_groups=mesh['dp_0'=8,'dp_1'=4,'dp_2'=2,'sy'=2,'sx'=2] {'dp_1'}, use_global_device_ids=true, to_apply=%region_56.57 | all-reduce | flops 128 | bytes 1024 | tf_op jit(solution)/shard_map/psum | solution.py:37
  274.6 10.3 %all-reduce.23 = (f32[64]{0:T(128)S(1)}, f32[64]{0:T(128)S(1)}) all-reduce(f32[64]{0:T(128)S(1)} %get-tuple-element.125, f32[64]{0:T(128)S(1)} %get-tuple-element.126), channel_id=1, replica_groups=mesh['dp_0'=8,'dp_1'=4,'dp_2'=2,'sy'=2,'sx'=2] {'sx'}, use_global_device_ids=true, to_apply=%region_59.60 | all-reduce | flops 128 | bytes 1024 | tf_op jit(solution)/shard_map/psum | solution.py:37
  295.8 7.9 %all-to-all-start.6 = ((bf16[64,2,128]{2,1,0:T(2,128)(2,1)}), bf16[64,2,128]{2,1,0:T(2,128)(2,1)S(1)}, u32[]{:S(2)}, u32[]{:S(2)}) async-start(bf16[64,2,128]{2,1,0:T(2,128)(2,1)} %reshape.1077), calls=%async_computation.6 | async-start | bytes 65536 | tf_op jit(solution)/shard_map/all_to_all | solution.py:27
  323.7 9.2 %all-to-all-done.4 = bf16[64,2,288]{2,1,0:T(2,128)(2,1)S(1)} async-done(((bf16[64,2,288]{2,1,0:T(2,128)(2,1)}), bf16[64,2,288]{2,1,0:T(2,128)(2,1)S(1)}, u32[]{:S(2)}, u32[]{:S(2)}) %all-to-all-start.4) | async-done | bytes 73760 | tf_op jit(solution)/shard_map/all_to_all | solution.py:27
  341.1 13.8 %all-reduce.4 = (f32[64]{0:T(128)S(1)}, f32[64]{0:T(128)S(1)}) all-reduce(f32[64]{0:T(128)S(1)} %get-tuple-element.14, f32[64]{0:T(128)S(1)} %get-tuple-element.13), channel_id=1, replica_groups=mesh['dp_0'=8,'dp_1'=4,'dp_2'=2,'sy'=2,'sx'=2] {'dp_0'}, use_global_device_ids=true, to_apply=%region_70.71 | all-reduce | flops 128 | bytes 1024 | tf_op jit(solution)/shard_map/psum | solution.py:37
  354.9 8.4 %all-reduce.13 = (f32[64]{0:T(128)S(1)}, f32[64]{0:T(128)S(1)}) all-reduce(f32[64]{0:T(128)S(1)} %get-tuple-element.69, f32[64]{0:T(128)S(1)} %get-tuple-element.70), channel_id=1, replica_groups=mesh['dp_0'=8,'dp_1'=4,'dp_2'=2,'sy'=2,'sx'=2] {'dp_1'}, use_global_device_ids=true, to_apply=%region_71.72 | all-reduce | flops 128 | bytes 1024 | tf_op jit(solution)/shard_map/psum | solution.py:37
  372.3 11.8 %all-reduce.22 = (f32[64]{0:T(128)S(1)}, f32[64]{0:T(128)S(1)}) all-reduce(f32[64]{0:T(128)S(1)} %get-tuple-element.123, f32[64]{0:T(128)S(1)} %get-tuple-element.124), channel_id=1, replica_groups=mesh['dp_0'=8,'dp_1'=4,'dp_2'=2,'sy'=2,'sx'=2] {'sx'}, use_global_device_ids=true, to_apply=%region_74.75 | all-reduce | flops 128 | bytes 1024 | tf_op jit(solution)/shard_map/psum | solution.py:37
  385.3 11.7 %all-reduce.3 = (f32[256]{0:T(256)S(1)}, f32[256]{0:T(256)S(1)}) all-reduce(f32[256]{0:T(256)S(1)} %get-tuple-element.6, f32[256]{0:T(256)S(1)} %get-tuple-element.5), channel_id=1, replica_groups=mesh['dp_0'=8,'dp_1'=4,'dp_2'=2,'sy'=2,'sx'=2] {'dp_0'}, use_global_device_ids=true, to_apply=%region_85.86 | all-reduce | flops 512 | bytes 4096 | tf_op jit(solution)/shard_map/psum | solution.py:37
  412.0 10.0 %all-reduce.21 = (f32[256]{0:T(256)S(1)}, f32[256]{0:T(256)S(1)}) all-reduce(f32[256]{0:T(256)S(1)} %get-tuple-element.121, f32[256]{0:T(256)S(1)} %get-tuple-element.122), channel_id=1, replica_groups=mesh['dp_0'=8,'dp_1'=4,'dp_2'=2,'sy'=2,'sx'=2] {'sx'}, use_global_device_ids=true, to_apply=%region_89.90 | all-reduce | flops 512 | bytes 4096 | tf_op jit(solution)/shard_map/psum | solution.py:37
  423.8 11.6 %all-reduce.2 = (f32[64]{0:T(128)S(1)}, f32[64]{0:T(128)S(1)}) all-reduce(f32[64]{0:T(128)S(1)} %get-tuple-element.12, f32[64]{0:T(128)S(1)} %get-tuple-element.11), channel_id=1, replica_groups=mesh['dp_0'=8,'dp_1'=4,'dp_2'=2,'sy'=2,'sx'=2] {'dp_0'}, use_global_device_ids=true, to_apply=%region_100.101 | all-reduce | flops 128 | bytes 1024 | tf_op jit(solution)/shard_map/psum | solution.py:37
  452.2 10.3 %all-reduce.20 = (f32[64]{0:T(128)S(1)}, f32[64]{0:T(128)S(1)}) all-reduce(f32[64]{0:T(128)S(1)} %get-tuple-element.119, f32[64]{0:T(128)S(1)} %get-tuple-element.120), channel_id=1, replica_groups=mesh['dp_0'=8,'dp_1'=4,'dp_2'=2,'sy'=2,'sx'=2] {'sx'}, use_global_device_ids=true, to_apply=%region_104.105 | all-reduce | flops 128 | bytes 1024 | tf_op jit(solution)/shard_map/psum | solution.py:37
  472.0 7.9 %all-to-all-start.7 = ((bf16[64,2,288]{2,1,0:T(2,128)(2,1)}), bf16[64,2,288]{2,1,0:T(2,128)(2,1)S(1)}, u32[]{:S(2)}, u32[]{:S(2)}) async-start(bf16[64,2,288]{2,1,0:T(2,128)(2,1)} %reshape.1079), calls=%async_computation.7 | async-start | bytes 196608 | tf_op jit(solution)/shard_map/all_to_all | solution.py:27
  513.5 14.1 %all-reduce.1 = (f32[64]{0:T(128)S(1)}, f32[64]{0:T(128)S(1)}) all-reduce(f32[64]{0:T(128)S(1)} %get-tuple-element.10, f32[64]{0:T(128)S(1)} %get-tuple-element.9), channel_id=1, replica_groups=mesh['dp_0'=8,'dp_1'=4,'dp_2'=2,'sy'=2,'sx'=2] {'dp_0'}, use_global_device_ids=true, to_apply=%region_115.116 | all-reduce | flops 128 | bytes 1024 | tf_op jit(solution)/shard_map/psum | solution.py:37
  527.6 8.1 %all-reduce.10 = (f32[64]{0:T(128)S(1)}, f32[64]{0:T(128)S(1)}) all-reduce(f32[64]{0:T(128)S(1)} %get-tuple-element.63, f32[64]{0:T(128)S(1)} %get-tuple-element.64), channel_id=1, replica_groups=mesh['dp_0'=8,'dp_1'=4,'dp_2'=2,'sy'=2,'sx'=2] {'dp_1'}, use_global_device_ids=true, to_apply=%region_116.117 | all-reduce | flops 128 | bytes 1024 | tf_op jit(solution)/shard_map/psum | solution.py:37
  544.7 10.2 %all-reduce.19 = (f32[64]{0:T(128)S(1)}, f32[64]{0:T(128)S(1)}) all-reduce(f32[64]{0:T(128)S(1)} %get-tuple-element.117, f32[64]{0:T(128)S(1)} %get-tuple-element.118), channel_id=1, replica_groups=mesh['dp_0'=8,'dp_1'=4,'dp_2'=2,'sy'=2,'sx'=2] {'sx'}, use_global_device_ids=true, to_apply=%region_119.120 | all-reduce | flops 128 | bytes 1024 | tf_op jit(solution)/shard_map/psum | solution.py:37
  556.1 11.7 %all-reduce = (f32[256]{0:T(256)S(1)}, f32[256]{0:T(256)S(1)}) all-reduce(f32[256]{0:T(256)S(1)} %get-tuple-element.4, f32[256]{0:T(256)S(1)} %get-tuple-element.3), channel_id=1, replica_groups=mesh['dp_0'=8,'dp_1'=4,'dp_2'=2,'sy'=2,'sx'=2] {'dp_0'}, use_global_device_ids=true, to_apply=%region_130.131 | all-reduce | flops 512 | bytes 4096 | tf_op jit(solution)/shard_map/psum | solution.py:37
  582.8 10.0 %all-reduce.18 = (f32[256]{0:T(256)S(1)}, f32[256]{0:T(256)S(1)}) all-reduce(f32[256]{0:T(256)S(1)} %get-tuple-element.115, f32[256]{0:T(256)S(1)} %get-tuple-element.116), channel_id=1, replica_groups=mesh['dp_0'=8,'dp_1'=4,'dp_2'=2,'sy'=2,'sx'=2] {'sx'}, use_global_device_ids=true, to_apply=%region_134.135 | all-reduce | flops 512 | bytes 4096 | tf_op jit(solution)/shard_map/psum | solution.py:37
  601.9 9.5 %all-to-all-start.11 = ((bf16[64,4,1000]{2,1,0:T(4,128)(2,1)}), bf16[64,4,1000]{2,1,0:T(4,128)(2,1)S(1)}, u32[]{:S(2)}, u32[]{:S(2)}) async-start(bf16[64,4,1000]{2,1,0:T(4,128)(2,1)} %broadcast_in_dim.58), calls=%async_computation.11 | async-start | bytes 1048576 | tf_op jit(solution)/shard_map/all_to_all | solution.py:27
  612.0 16.0 %all-to-all-done.11 = bf16[64,4,1000]{2,1,0:T(4,128)(2,1)S(1)} async-done(((bf16[64,4,1000]{2,1,0:T(4,128)(2,1)}), bf16[64,4,1000]{2,1,0:T(4,128)(2,1)S(1)}, u32[]{:S(2)}, u32[]{:S(2)}) %all-to-all-start.11) | async-done | bytes 512032 | tf_op jit(solution)/shard_map/all_to_all | solution.py:27
  639.3 9.9 %all-to-all-done.12 = f32[64,1,1]{2,1,0:T(1,128)S(1)} async-done(((f32[64,1,1]{2,1,0:T(1,128)}), f32[64,1,1]{2,1,0:T(1,128)S(1)}, u32[]{:S(2)}, u32[]{:S(2)}) %all-to-all-start.12) | async-done | bytes 288 | tf_op jit(solution)/shard_map/all_to_all | solution.py:27
  (391 shorter events, 279.6 us)
Async XLA Ops:
  16.7 33.4 %all-to-all-start = ((bf16[64,2,128]{2,1,0:T(2,128)(2,1)}), bf16[64,2,128]{2,1,0:T(2,128)(2,1)S(1)}, u32[]{:S(2)}, u32[]{:S(2)}) async-start(bf16[64,2,128]{2,1,0:T(2,128)(2,1)} %reshape.1069), calls=%async_computation | async-start | bytes 65536 | tf_op jit(solution)/shard_map/all_to_all | solution.py:27
  49.3 56.0 %copy-start.28 = (f32[64]{0:T(128)}, f32[64]{0:T(128)S(1)}, u32[]{:S(2)}) copy-start(f32[64]{0:T(128)S(1)} %get-tuple-element.225) | copy-start | bytes 772
  49.3 56.0 %copy-start.30 = (f32[64]{0:T(128)}, f32[64]{0:T(128)S(1)}, u32[]{:S(2)}) copy-start(f32[64]{0:T(128)S(1)} %get-tuple-element.265) | copy-start | bytes 772
  49.3 235.7 %copy-start.24 = (f32[64]{0:T(128)}, f32[64]{0:T(128)S(1)}, u32[]{:S(2)}) copy-start(f32[64]{0:T(128)S(1)} %get-tuple-element.223) | copy-start | bytes 772
  50.1 70.0 %all-to-all-start.2 = ((bf16[64,2,128]{2,1,0:T(2,128)(2,1)}), bf16[64,2,128]{2,1,0:T(2,128)(2,1)S(1)}, u32[]{:S(2)}, u32[]{:S(2)}) async-start(bf16[64,2,128]{2,1,0:T(2,128)(2,1)} %reshape.1067), calls=%async_computation.2 | async-start | bytes 65536 | tf_op jit(solution)/shard_map/all_to_all | solution.py:27
  106.2 5.6 collective-permute-start
  110.5 4.4 collective-permute-start.1
  115.1 30.9 %collective-permute-start.2 = (bf16[1,30,1,64]{3,2,1,0:T(2,128)(2,1)S(1)}, bf16[1,30,1,64]{3,2,1,0:T(2,128)(2,1)S(1)}, u32[]{:S(2)}, u32[]{:S(2)}) collective-permute-start(bf16[1,30,1,64]{3,2,1,0:T(2,128)(2,1)S(1)} %get-tuple-element.185), channel_id=1, source_target_pairs={{0,1},{2,3},{4,5},{6,7},{8,9},{10,11},{12,13},{14,15},{16,17},{18,... | collective-permute-start | bytes 11528 | tf_op jit(solution)/shard_map/ppermute | solution.py:48
  116.4 29.6 %collective-permute-start.3 = (bf16[1,30,1,64]{3,2,1,0:T(2,128)(2,1)S(1)}, bf16[1,30,1,64]{3,2,1,0:T(2,128)(2,1)S(1)}, u32[]{:S(2)}, u32[]{:S(2)}) collective-permute-start(bf16[1,30,1,64]{3,2,1,0:T(2,128)(2,1)S(1)} %get-tuple-element.184), channel_id=1, source_target_pairs={{1,0},{3,2},{5,4},{7,6},{9,8},{11,10},{13,12},{15,14},{17,16},{19,... | collective-permute-start | bytes 11528 | tf_op jit(solution)/shard_map/ppermute | solution.py:50
  120.1 19.3 %all-to-all-start.3 = ((bf16[64,2,128]{2,1,0:T(2,128)(2,1)}), bf16[64,2,128]{2,1,0:T(2,128)(2,1)S(1)}, u32[]{:S(2)}, u32[]{:S(2)}) async-start(bf16[64,2,128]{2,1,0:T(2,128)(2,1)} %reshape.1073), calls=%async_computation.3 | async-start | bytes 65536 | tf_op jit(solution)/shard_map/all_to_all | solution.py:27
  139.4 16.5 %all-to-all-start.1 = ((bf16[64,2,288]{2,1,0:T(2,128)(2,1)}), bf16[64,2,288]{2,1,0:T(2,128)(2,1)}, u32[]{:S(2)}, u32[]{:S(2)}) async-start(bf16[64,2,288]{2,1,0:T(2,128)(2,1)} %reshape.1071), calls=%async_computation.1 | async-start | bytes 196608 | tf_op jit(solution)/shard_map/all_to_all | solution.py:27
  156.0 139.9 %all-to-all-start.5 = ((bf16[64,2,128]{2,1,0:T(2,128)(2,1)}), bf16[64,2,128]{2,1,0:T(2,128)(2,1)S(1)}, u32[]{:S(2)}, u32[]{:S(2)}) async-start(bf16[64,2,128]{2,1,0:T(2,128)(2,1)} %reshape.1065), calls=%async_computation.5 | async-start | bytes 65536 | tf_op jit(solution)/shard_map/all_to_all | solution.py:27
  207.2 37.1 %copy-start.47 = (f32[1,256]{1,0:T(1,128)S(1)}, f32[1,256]{1,0:T(1,128)}, u32[]{:S(2)}) copy-start(f32[1,256]{1,0:T(1,128)} %get-tuple-element.213) | copy-start | bytes 3076
  286.0 6.7 %collective-permute-start.4 = (bf16[1,1,28,64]{3,2,1,0:T(8,128)(2,1)S(1)}, bf16[1,1,28,64]{3,2,1,0:T(8,128)(2,1)S(1)}, u32[]{:S(2)}, u32[]{:S(2)}) collective-permute-start(bf16[1,1,28,64]{3,2,1,0:T(8,128)(2,1)S(1)} %get-tuple-element.195), channel_id=1, source_target_pairs={{0,2},{1,3},{4,6},{5,7},{8,10},{9,11},{12,14},{13,15},{16,18},{17,... | collective-permute-start | bytes 10760 | tf_op jit(solution)/shard_map/ppermute | solution.py:48
  291.3 4.4 collective-permute-start.5
  295.8 18.7 %all-to-all-start.6 = ((bf16[64,2,128]{2,1,0:T(2,128)(2,1)}), bf16[64,2,128]{2,1,0:T(2,128)(2,1)S(1)}, u32[]{:S(2)}, u32[]{:S(2)}) async-start(bf16[64,2,128]{2,1,0:T(2,128)(2,1)} %reshape.1077), calls=%async_computation.6 | async-start | bytes 65536 | tf_op jit(solution)/shard_map/all_to_all | solution.py:27
  303.8 34.2 %collective-permute-start.6 = (bf16[1,30,1,64]{3,2,1,0:T(2,128)(2,1)S(1)}, bf16[1,30,1,64]{3,2,1,0:T(2,128)(2,1)S(1)}, u32[]{:S(2)}, u32[]{:S(2)}) collective-permute-start(bf16[1,30,1,64]{3,2,1,0:T(2,128)(2,1)S(1)} %get-tuple-element.180), channel_id=1, source_target_pairs={{0,1},{2,3},{4,5},{6,7},{8,9},{10,11},{12,13},{14,15},{16,17},{18,... | collective-permute-start | bytes 11528 | tf_op jit(solution)/shard_map/ppermute | solution.py:48
  305.1 32.9 %collective-permute-start.7 = (bf16[1,30,1,64]{3,2,1,0:T(2,128)(2,1)S(1)}, bf16[1,30,1,64]{3,2,1,0:T(2,128)(2,1)S(1)}, u32[]{:S(2)}, u32[]{:S(2)}) collective-permute-start(bf16[1,30,1,64]{3,2,1,0:T(2,128)(2,1)S(1)} %get-tuple-element.179), channel_id=1, source_target_pairs={{1,0},{3,2},{5,4},{7,6},{9,8},{11,10},{13,12},{15,14},{17,16},{19,... | collective-permute-start | bytes 11528 | tf_op jit(solution)/shard_map/ppermute | solution.py:50
  314.6 18.3 %all-to-all-start.4 = ((bf16[64,2,288]{2,1,0:T(2,128)(2,1)}), bf16[64,2,288]{2,1,0:T(2,128)(2,1)S(1)}, u32[]{:S(2)}, u32[]{:S(2)}) async-start(bf16[64,2,288]{2,1,0:T(2,128)(2,1)} %reshape.1075), calls=%async_computation.4 | async-start | bytes 196608 | tf_op jit(solution)/shard_map/all_to_all | solution.py:27
  332.9 139.1 %all-to-all-start.8 = ((bf16[64,2,128]{2,1,0:T(2,128)(2,1)}), bf16[64,2,128]{2,1,0:T(2,128)(2,1)S(1)}, u32[]{:S(2)}, u32[]{:S(2)}) async-start(bf16[64,2,128]{2,1,0:T(2,128)(2,1)} %reshape.1063), calls=%async_computation.8 | async-start | bytes 65536 | tf_op jit(solution)/shard_map/all_to_all | solution.py:27
  340.7 43.4 %copy-start.6 = (bf16[64,4,64]{2,1,0:T(4,128)(2,1)S(1)}, bf16[64,4,64]{2,1,0:T(4,128)(2,1)}, u32[]{:S(2)}) copy-start(bf16[64,4,64]{2,1,0:T(4,128)(2,1)} %reshape.1066) | copy-start | bytes 98308
  463.5 5.2 collective-permute-start.8
  467.5 4.4 collective-permute-start.9
  472.0 19.1 %all-to-all-start.7 = ((bf16[64,2,288]{2,1,0:T(2,128)(2,1)}), bf16[64,2,288]{2,1,0:T(2,128)(2,1)S(1)}, u32[]{:S(2)}, u32[]{:S(2)}) async-start(bf16[64,2,288]{2,1,0:T(2,128)(2,1)} %reshape.1079), calls=%async_computation.7 | async-start | bytes 196608 | tf_op jit(solution)/shard_map/all_to_all | solution.py:27
  479.9 21.7 %collective-permute-start.10 = (bf16[1,30,1,64]{3,2,1,0:T(2,128)(2,1)S(1)}, bf16[1,30,1,64]{3,2,1,0:T(2,128)(2,1)S(1)}, u32[]{:S(2)}, u32[]{:S(2)}) collective-permute-start(bf16[1,30,1,64]{3,2,1,0:T(2,128)(2,1)S(1)} %get-tuple-element.175), channel_id=1, source_target_pairs={{0,1},{2,3},{4,5},{6,7},{8,9},{10,11},{12,13},{14,15},{16,17},{18,... | collective-permute-start | bytes 11528 | tf_op jit(solution)/shard_map/ppermute | solution.py:48
  481.2 20.4 %collective-permute-start.11 = (bf16[1,30,1,64]{3,2,1,0:T(2,128)(2,1)S(1)}, bf16[1,30,1,64]{3,2,1,0:T(2,128)(2,1)S(1)}, u32[]{:S(2)}, u32[]{:S(2)}) collective-permute-start(bf16[1,30,1,64]{3,2,1,0:T(2,128)(2,1)S(1)} %get-tuple-element.174), channel_id=1, source_target_pairs={{1,0},{3,2},{5,4},{7,6},{9,8},{11,10},{13,12},{15,14},{17,16},{19,... | collective-permute-start | bytes 11528 | tf_op jit(solution)/shard_map/ppermute | solution.py:50
  492.4 101.3 %all-to-all-start.10 = ((f32[64,1,3000]{2,1,0:T(1,128)}), f32[64,1,3000]{2,1,0:T(1,128)S(1)}, u32[]{:S(2)}, u32[]{:S(2)}) async-start(f32[64,1,3000]{2,1,0:T(1,128)} %broadcast_in_dim.57), calls=%async_computation.10 | async-start | bytes 1572864 | tf_op jit(solution)/shard_map/all_to_all | solution.py:27
  513.0 41.9 %copy-start.5 = (bf16[64,4,64]{2,1,0:T(4,128)(2,1)S(1)}, bf16[64,4,64]{2,1,0:T(4,128)(2,1)}, u32[]{:S(2)}) copy-start(bf16[64,4,64]{2,1,0:T(4,128)(2,1)} %reshape.1064) | copy-start | bytes 98308
  555.6 37.1 %copy-start.49 = (f32[1,256]{1,0:T(1,128)S(1)}, f32[1,256]{1,0:T(1,128)}, u32[]{:S(2)}) copy-start(f32[1,256]{1,0:T(1,128)} %get-tuple-element.214) | copy-start | bytes 3076
  594.3 6.6 %all-to-all-start.9 = ((f32[4,1,256]{2,1,0:T(1,128)}), f32[4,1,256]{2,1,0:T(1,128)S(1)}, u32[]{:S(2)}, u32[]{:S(2)}) async-start(f32[4,1,256]{2,1,0:T(1,128)} %broadcast_in_dim.56), calls=%async_computation.9 | async-start | bytes 8192 | tf_op jit(solution)/shard_map/all_to_all | solution.py:27
  601.9 26.2 %all-to-all-start.11 = ((bf16[64,4,1000]{2,1,0:T(4,128)(2,1)}), bf16[64,4,1000]{2,1,0:T(4,128)(2,1)S(1)}, u32[]{:S(2)}, u32[]{:S(2)}) async-start(bf16[64,4,1000]{2,1,0:T(4,128)(2,1)} %broadcast_in_dim.58), calls=%async_computation.11 | async-start | bytes 1048576 | tf_op jit(solution)/shard_map/all_to_all | solution.py:27
  631.0 18.3 %all-to-all-start.12 = ((f32[64,1,1]{2,1,0:T(1,128)}), f32[64,1,1]{2,1,0:T(1,128)S(1)}, u32[]{:S(2)}, u32[]{:S(2)}) async-start(f32[64,1,1]{2,1,0:T(1,128)} %broadcast_in_dim.60), calls=%async_computation.12 | async-start | bytes 65536 | tf_op jit(solution)/shard_map/all_to_all | solution.py:27
  (55 other events, 161.9 us)
where the time goes:
time: 656 us; the launch traced here: 653 us
  blocking collectives  357 us (54%)
  starting transfers between devices  128 us (20%)
  waiting for transfers between devices  69.3 us (11%)
  local copies, waits for them, and re-layouts  47.5 us (7%)
  between operations  26.9 us (4%)
  other arithmetic  20.2 us (3%)
    psum x45, blocking collectives, one_axis_at_a_time(): return functools.reduce(lax.psum, axes, value)  357 us
    all_to_all x13, starting transfers between devices, copy_for_each(): lax.all_to_all(jnp.broadcast_to(value[None], (length, *value.shape)), axi...  103 us
    all_to_all x13, waiting for transfers between devices, copy_for_each(): lax.all_to_all(jnp.broadcast_to(value[None], (length, *value.shape)), axi...  60 us
    unnamed x176, local copies, waits for them, and re-layouts  27 us
    ppermute x6, starting transfers between devices, extended(): lax.ppermute(head, axis, [((i + 1) % count, i) for i in range(ends)])  15.6 us
  transfers between devices with their start and end apart: 25, of which 11 were waited for; matrix products, arithmetic and copies ran while one was open for 8% of the time, Pallas kernels for 0%

commit v1 on v0

v1 whole, which is shorter than its diff:
```python
import functools

import jax
import jax.numpy as jnp
from jax import lax
from jax.experimental import pallas as pl
from jax.experimental.pallas import tpu as pltpu
from jax.sharding import Mesh
from jax.sharding import PartitionSpec as P

BLOCKS = 3
GRID = 50
EPS_NORM = 1e-06
EPS_BN = 1e-05
FEAT = 256
MID = 64
CLASSES = 1000
TILE = 28
OWN = TILE * TILE
SIDE = 32
CELLS = SIDE * SIDE
OWN_ROWS = TILE * SIDE
HALO = SIDE - TILE
DP = ("z", "y", "xh")
ALL = ("z", "y", "xh", "sy", "sx")
TILES = 4
IMAGES = 64

PARAMS = pltpu.CompilerParams(vmem_limit_bytes=32 * 1024 * 1024)
VM = pl.BlockSpec(memory_space=pltpu.VMEM)
SM = pl.BlockSpec(memory_space=pltpu.SMEM)


def own_cells(channels):
    cell = lax.broadcasted_iota(jnp.int32, (OWN_ROWS, channels), 0)
    return (cell & (SIDE - 1)) < TILE


def moments(y):
    own = own_cells(y.shape[1])
    top = y[:OWN_ROWS]
    mean = jnp.sum(jnp.where(own, top, 0.0), axis=0, keepdims=True) * (1.0 / OWN)
    off = jnp.where(own, top - mean, 0.0)
    return jnp.concatenate([mean, jnp.sum(off * off, axis=0, keepdims=True)], axis=1)


def merged(parts, cells):
    count, width = parts.shape[0], parts.shape[1] // 2
    means = parts[:, :width]
    mean = jnp.sum(means, axis=0, keepdims=True) * (1.0 / count)
    off = means - mean
    squares = jnp.sum(parts[:, width:] + cells * (off * off), axis=0, keepdims=True)
    return mean, squares


def normalizer(parts, gain, shift, cells):
    mean, squares = merged(parts, cells)
    scale = lax.rsqrt(squares * (1.0 / (cells * parts.shape[0])) + EPS_BN) * gain
    return lambda y: (y - mean) * scale + shift


def dot_t(left, right):
    return lax.dot_general(
        left, right, (((1,), (1,)), ((), ())), preferred_element_type=jnp.float32
    )


def emit(y, y_ref, out_ref):
    y_ref[...] = y
    out_ref[...] = jnp.broadcast_to(moments(y), out_ref.shape)


def reduce_kernel(x_ref, w_ref, y_ref, out_ref):
    emit(dot_t(x_ref[...], w_ref[...]), y_ref, out_ref)


def spatial_kernel(cells, at_ref, parts_ref, y_ref, gain_ref, shift_ref, w_ref, y2_ref, out_ref, frame):
    norm = normalizer(parts_ref[...], gain_ref[...], shift_ref[...], cells)
    a = jnp.maximum(norm(y_ref[...]), 0.0)
    sy, sx = at_ref[0], at_ref[1]
    cell = lax.broadcasted_iota(jnp.int32, (CELLS, MID), 0)
    col = cell & (SIDE - 1)
    row = ((cell + jnp.where((sx == 1) & (col > TILE), SIDE, 0)) >> 5) & (SIDE - 1)
    inside = (row != SIDE - 1 - 3 * sy) & (col != SIDE - 1 - 3 * sx)
    a = jnp.where(inside, a, 0.0)
    both = jnp.concatenate(
        [pltpu.roll(a, 1, 0), a, pltpu.roll(a, CELLS - 1, 0)], axis=1
    ).astype(jnp.bfloat16)
    frame[SIDE : SIDE + CELLS, :] = both
    frame[0:SIDE, :] = both[CELLS - SIDE :]
    frame[SIDE + CELLS :, :] = both[:SIDE]
    total = None
    for i in range(3):
        term = dot_t(frame[SIDE * i : SIDE * i + CELLS, :], w_ref[:, 3 * MID * i : 3 * MID * (i + 1)])
        total = term if total is None else total + term
    emit(total, y2_ref, out_ref)


def expand_kernel(cells, parts_ref, y_ref, gain_ref, shift_ref, w_ref, y3_ref, out_ref):
    norm = normalizer(parts_ref[...], gain_ref[...], shift_ref[...], cells)
    c = jnp.maximum(norm(y_ref[...]), 0.0).astype(jnp.bfloat16)
    emit(dot_t(c, w_ref[...]), y3_ref, out_ref)


def block_kernel(cells, parts_ref, y_ref, gain_ref, shift_ref, x_ref, w_ref, new_ref, y1_ref, out_ref):
    norm = normalizer(parts_ref[...], gain_ref[...], shift_ref[...], cells)
    new = jnp.maximum(x_ref[...].astype(jnp.float32) + norm(y_ref[...]), 0.0).astype(jnp.bfloat16)
    new_ref[...] = new
    emit(dot_t(new, w_ref[...]), y1_ref, out_ref)


def last_kernel(cells, parts_ref, y_ref, gain_ref, shift_ref, x_ref, new_ref, out_ref):
    norm = normalizer(parts_ref[...], gain_ref[...], shift_ref[...], cells)
    top = x_ref[:OWN_ROWS, :].astype(jnp.float32) + norm(y_ref[:OWN_ROWS, :])
    new = jnp.maximum(top, 0.0).astype(jnp.bfloat16)
    for row in range(TILE):
        new_ref[row] = new[SIDE * row : SIDE * row + TILE]
    kept = jnp.where(own_cells(FEAT), new.astype(jnp.float32), 0.0)
    out_ref[...] = jnp.broadcast_to(jnp.sum(kept, axis=0, keepdims=True), out_ref.shape)


def call(kernel, outs, *args, scratch=(), smem=0):
    return pl.pallas_call(
        kernel,
        out_shape=[jax.ShapeDtypeStruct(s, d) for s, d in outs],
        in_specs=[SM] * smem + [VM] * (len(args) - smem),
        out_specs=[VM] * len(outs),
        scratch_shapes=list(scratch),
        compiler_params=PARAMS,
    )(*args)


def tile_frame(features, sy, sx):
    own = features[0]
    cols = jnp.where(sx == 0, own[:, TILE - HALO :], own[:, :HALO])
    rows = jnp.where(sy == 0, own[TILE - HALO :], own[:HALO])
    corner = jnp.where(sx == 0, rows[:, TILE - HALO :], rows[:, :HALO])
    cols = lax.ppermute(cols, "sx", [(0, 1), (1, 0)])
    rows = lax.ppermute(rows, "sy", [(0, 1), (1, 0)])
    corner = lax.ppermute(corner, ("sy", "sx"), [(i, 3 - i) for i in range(4)])
    right = jnp.concatenate([cols, corner], axis=0)
    right = jnp.where(sx == 1, jnp.concatenate([right[1:], right[:1]], axis=0), right)
    left = jnp.concatenate([own, rows], axis=0)
    return jnp.concatenate([left, right], axis=1).reshape(CELLS, FEAT)


def norm_ratio(base, direction, axis):
    square = lambda v: jnp.sum(v * v, axis=axis, keepdims=True)
    return jnp.sqrt(square(base)) / jnp.sqrt(square(direction) + EPS_NORM)


def perturbed(base, dir_a, dir_b, alpha, axis):
    base, dir_a, dir_b = (v.astype(jnp.float32) for v in (base, dir_a, dir_b))
    value = (
        base
        + alpha[0] * norm_ratio(base, dir_a, axis) * dir_a
        + alpha[1] * norm_ratio(base, dir_b, axis) * dir_b
    )
    return value.astype(jnp.bfloat16)


def spread(row, axes):
    count, width = lax.axis_size(axes), row.size
    pieces = jnp.broadcast_to(row.reshape(1, -1, 128), (count, width // 128, 128))
    return lax.all_to_all(pieces, axes, 0, 0, tiled=True).reshape(count, width)


def per_device(
    features,
    labels,
    grid,
    w_reduce,
    w_spatial,
    w_expand,
    w_class,
    dir_reduce,
    dir_spatial,
    dir_expand,
    dir_class,
    gain_mid,
    shift_mid,
    gain_out,
    shift_out,
):
    sy, sx = lax.axis_index("sy"), lax.axis_index("sx")
    at = jnp.stack([sy, sx]).astype(jnp.int32)
    alpha = (2.0 * grid.astype(jnp.float32) + 1.0 - GRID) / GRID

    with jax.named_scope("filters"):
        p_reduce = perturbed(
            w_reduce[:, :, 0], dir_reduce[0, :, :, 0], dir_reduce[1, :, :, 0], alpha, 1
        )
        first = spread(p_reduce[0], DP)
        p_spatial = perturbed(
            w_spatial[..., 0], dir_spatial[0, ..., 0], dir_spatial[1, ..., 0], alpha, (1, 2, 3)
        ).reshape(BLOCKS, -1)
        p_expand = perturbed(w_expand, dir_expand[0], dir_expand[1], alpha, 1)
        p_expand = jnp.swapaxes(p_expand, 1, 2).reshape(BLOCKS, -1)
        rest = jnp.concatenate([p_reduce[1:].ravel(), p_spatial.ravel(), p_expand.ravel()])
        rest = jnp.pad(rest, (0, -rest.size % 128))

    with jax.named_scope("halo"):
        x = tile_frame(features, sy, sx)

    with jax.named_scope("filters"):
        (y1, sent) = call(
            reduce_kernel, [((CELLS, MID), jnp.float32), ((1, 2 * MID), jnp.float32)], x, first
        )
        every = spread(rest, DP)
        w_r = [first, every[:, :FEAT], every[:, FEAT : 2 * FEAT]]
        at_s, at_e = 2 * FEAT, 2 * FEAT + BLOCKS * 9 * MID
        w_s = [every[:, at_s + b * 9 * MID : at_s + (b + 1) * 9 * MID] for b in range(BLOCKS)]
        w_e = [
            every[:, at_e + b * 4 * MID : at_e + (b + 1) * 4 * MID].reshape(FEAT, MID)
            for b in range(BLOCKS)
        ]

    with jax.named_scope("class"):
        square = lambda v: jnp.sum(jnp.square(v.astype(jnp.float32)), axis=0)
        norms = jnp.concatenate([square(w_class), square(dir_class[0]), square(dir_class[1])])
        norms = jnp.sum(spread(jnp.pad(norms, (0, 72)), DP), axis=0)[: 3 * CLASSES]
        norms = jnp.sqrt(norms.reshape(3, CLASSES) + jnp.array([0.0, EPS_NORM, EPS_NORM])[:, None])
        p_class = (
            w_class.astype(jnp.float32)
            + alpha[0] * (norms[0] / norms[1]) * dir_class[0].astype(jnp.float32)
            + alpha[1] * (norms[0] / norms[2]) * dir_class[1].astype(jnp.float32)
        ).astype(jnp.bfloat16)
        p_class = spread(jnp.pad(p_class, ((0, 0), (0, 24))), DP).reshape(FEAT, 1024)

    exchange = lambda row: spread(row, ALL)
    row = lambda v: v.reshape(1, -1)
    for b in range(BLOCKS):
        with jax.named_scope(f"block_{b}"):
            y2, sent = call(
                functools.partial(spatial_kernel, OWN),
                [((CELLS, MID), jnp.float32), ((1, 2 * MID), jnp.float32)],
                at, exchange(sent), y1, row(gain_mid[b, 0]), row(shift_mid[b, 0]), w_s[b],
                scratch=[pltpu.VMEM((CELLS + 2 * SIDE, 3 * MID), jnp.bfloat16)], smem=1,
            )
            y3, sent = call(
                functools.partial(expand_kernel, OWN),
                [((CELLS, FEAT), jnp.float32), ((1, 2 * FEAT), jnp.float32)],
                exchange(sent), y2, row(gain_mid[b, 1]), row(shift_mid[b, 1]), w_e[b],
            )
            args = (exchange(sent), y3, row(gain_out[b]), row(shift_out[b]), x)
            if b < BLOCKS - 1:
                x, y1, sent = call(
                    functools.partial(block_kernel, OWN),
                    [((CELLS, FEAT), jnp.bfloat16), ((CELLS, MID), jnp.float32), ((1, 2 * MID), jnp.float32)],
                    *args, w_r[b + 1],
                )
            else:
                section, pooled = call(
                    functools.partial(last_kernel, OWN),
                    [((TILE, TILE, FEAT), jnp.bfloat16), ((1, FEAT), jnp.float32)],
                    *args,
                )
    with jax.named_scope("loss"):
        tag = jnp.broadcast_to(labels.astype(jnp.float32)[None], (1, 128))
        every = spread(jnp.concatenate([pooled, tag, tag], axis=1), ALL).reshape(IMAGES, TILES, -1)
        pooled = (jnp.sum(every[:, :, :FEAT], axis=1) / (OWN * TILES)).astype(jnp.bfloat16)
        tags = every[:, 0, FEAT].astype(jnp.int32)
        logits = jnp.dot(pooled, p_class, preferred_element_type=jnp.float32)[:, :CLASSES]
        summed = jnp.log(jnp.sum(jnp.exp(logits), axis=1))
        classes = lax.broadcasted_iota(jnp.int32, logits.shape, 1)
        picked = jnp.sum(jnp.where(classes == tags[:, None], logits, 0.0), axis=1)
        losses = summed - picked
        mean_loss = jnp.sum(losses) / IMAGES
        image_loss = lax.dynamic_slice(losses, (lax.axis_index(DP),), (1,))
    return section[None], image_loss, mean_loss


def solution(mesh):
    split = Mesh(
        mesh.devices.reshape(8, 4, 2, mesh.shape["sy"], mesh.shape["sx"]), ALL
    )
    tiles = P(DP, "sy", "sx", None)
    return jax.shard_map(
        per_device,
        mesh=split,
        in_specs=(
            tiles,
            P(DP),
            P(),
            P(None, None, DP),
            P(None, None, None, None, DP),
            P(None, None, DP),
            P(DP, None),
            P(None, None, None, DP),
            P(None, None, None, None, None, DP),
            P(None, None, None, DP),
            P(None, DP, None),
            P(),
            P(),
            P(),
            P(),
        ),
        out_specs=(tiles, P(DP), P()),
        check_vma=False,
    )
```

time: 656 us -> 352 us (0.54)
  blocking collectives: 357 us -> 63.2 us
  waiting for transfers between devices: 69.3 us -> 164 us
  starting transfers between devices: 128 us -> 82.9 us
  local copies, waits for them, and re-layouts: 47.5 us -> 15.8 us
  between operations: 26.9 us -> 3.55 us
  Pallas kernels: 0 us -> 10.6 us
  other arithmetic: 20.2 us -> 9.85 us
    psum x45 -> x0, blocking collectives: 357 us -> none  [one_axis_at_a_time(): return functools.reduce(lax.psum, axes, value)]
    all_to_all x13 -> x11, waiting for transfers between devices: 60 us -> 164 us  [spread(): return lax.all_to_all(pieces, axes, 0, 0, tiled=True).reshape(count, width)]
    all_to_all x0 -> x3, blocking collectives: none -> 63.2 us  [spread(): return lax.all_to_all(pieces, axes, 0, 0, tiled=True).reshape(count, width)]
    all_to_all x13 -> x11, starting transfers between devices: 103 us -> 77.7 us  [spread(): return lax.all_to_all(pieces, axes, 0, 0, tiled=True).reshape(count, width)]
    unnamed x176 -> x40, local copies, waits for them, and re-layouts: 27 us -> 3.63 us
    ppermute x12 -> x3, starting transfers between devices: 25.2 us -> 5.14 us  [the longest x1 2.92 us: tile_frame(): corner = lax.ppermute(corner, ('sy', 'sx'), [(i, 3 - i) for i in range(4)])]
    concatenate x55 -> x3, local copies, waits for them, and re-layouts: 12 us -> 0.18 us  [the longest x1 0.09 us: per_device(): jnp.concatenate([p_reduce[1:].ravel(), p_spatial.ravel(), p_expand.ravel()])]
    pallas_call x0 -> x10, Pallas kernels: none -> 10.6 us  [call(): pl.pallas_call(kernel, out_shape=[jax.ShapeDtypeStruct(s, d) for s, d in...]
  transfers between devices with their start and end apart: 25 -> 14, of which waited for: 11 -> 11; matrix products, arithmetic and copies ran while one was open for 8% -> 3% of each run, Pallas kernels for 0% -> 1%
where the time goes in v1:
time: 352 us; the launch traced here: 350 us
  waiting for transfers between devices  164 us (47%)
  starting transfers between devices  82.9 us (24%)
  blocking collectives  63.2 us (18%)
  local copies, waits for them, and re-layouts  15.8 us (4%)
  Pallas kernels  10.6 us (3%)
  other arithmetic  9.85 us (3%)
  between operations  3.55 us (1%)
    all_to_all x11, waiting for transfers between devices, spread(): return lax.all_to_all(pieces, axes, 0, 0, tiled=True).reshape(count, width)  164 us
    all_to_all x11, starting transfers between devices, spread(): return lax.all_to_all(pieces, axes, 0, 0, tiled=True).reshape(count, width)  77.7 us
    all_to_all x3, blocking collectives, spread(): return lax.all_to_all(pieces, axes, 0, 0, tiled=True).reshape(count, width)  63.2 us
    pallas_call x10, Pallas kernels, call(): pl.pallas_call(kernel, out_shape=[jax.ShapeDtypeStruct(s, d) for s, d in...  10.6 us
    broadcast_in_dim x17, local copies, waits for them, and re-layouts, spread(): jnp.broadcast_to(row.reshape(1, -1, 128), (count, width // 128, 128))  9.06 us
  transfers between devices with their start and end apart: 14, of which 11 were waited for; matrix products, arithmetic and copies ran while one was open for 3% of the time, Pallas kernels for 1%

profile of v1, /device:TPU:1, one launch (start us, length us, event | category | flops | bytes accessed | tf_op | source)
XLA Modules:
  0.0 350.5 jit_solution(16526824147903362290)
XLA Ops:
  1.5 2.1 collective-permute-start
  3.7 2.9 collective-permute-start.2
  11.1 12.7 %all-to-all-start = ((bf16[64,2,128]{2,1,0:T(2,128)(2,1)}), bf16[64,2,128]{2,1,0:T(2,128)(2,1)S(1)}, u32[]{:S(2)}, u32[]{:S(2)}) async-start(bf16[64,2,128]{2,1,0:T(2,128)(2,1)} %broadcast_in_dim.130), calls=%async_computation | async-start | bytes 65536 | tf_op jit(solution)/shard_map/filters/all_to_all | solution.py:165
  28.5 6.0 %all-to-all-done = bf16[64,2,128]{2,1,0:T(2,128)(2,1)S(1)} async-done(((bf16[64,2,128]{2,1,0:T(2,128)(2,1)}), bf16[64,2,128]{2,1,0:T(2,128)(2,1)S(1)}, u32[]{:S(2)}, u32[]{:S(2)}) %all-to-all-start) | async-done | bytes 32800 | tf_op jit(solution)/shard_map/filters/all_to_all | solution.py:165
  35.4 6.3 %all-to-all-start.2 = ((bf16[64,24,128]{2,1,0:T(8,128)(2,1)}), bf16[64,24,128]{2,1,0:T(8,128)(2,1)S(1)}, u32[]{:S(2)}, u32[]{:S(2)}) async-start(bf16[64,24,128]{2,1,0:T(8,128)(2,1)} %broadcast_in_dim.134), calls=%async_computation.2 | async-start | bytes 786432 | tf_op jit(solution)/shard_map/filters/all_to_all | solution.py:165
  42.6 13.6 %all-to-all-done.2 = bf16[64,24,128]{2,1,0:T(8,128)(2,1)S(1)} async-done(((bf16[64,24,128]{2,1,0:T(8,128)(2,1)}), bf16[64,24,128]{2,1,0:T(8,128)(2,1)S(1)}, u32[]{:S(2)}, u32[]{:S(2)}) %all-to-all-start.2) | async-done | bytes 393248 | tf_op jit(solution)/shard_map/filters/all_to_all | solution.py:165
  56.9 8.2 %all-to-all-start.1 = ((f32[256,1,128]{2,1,0:T(1,128)}), f32[256,1,128]{2,1,0:T(1,128)S(1)}, u32[]{:S(2)}, u32[]{:S(2)}) async-start(f32[256,1,128]{2,1,0:T(1,128)} %broadcast_in_dim.132), calls=%async_computation.1 | async-start | bytes 262144 | tf_op jit(solution)/shard_map/block_0/all_to_all | solution.py:165
  65.4 12.7 %all-to-all-done.1 = f32[256,1,128]{2,1,0:T(1,128)S(1)} async-done(((f32[256,1,128]{2,1,0:T(1,128)}), f32[256,1,128]{2,1,0:T(1,128)S(1)}, u32[]{:S(2)}, u32[]{:S(2)}) %all-to-all-start.1) | async-done | bytes 131104 | tf_op jit(solution)/shard_map/block_0/all_to_all | solution.py:165
  78.1 1.8 block_0.3
  80.5 5.5 %all-to-all-start.3 = ((f32[256,1,128]{2,1,0:T(1,128)}), f32[256,1,128]{2,1,0:T(1,128)S(1)}, u32[]{:S(2)}, u32[]{:S(2)}) async-start(f32[256,1,128]{2,1,0:T(1,128)} %broadcast_in_dim.136), calls=%async_computation.3 | async-start | bytes 262144 | tf_op jit(solution)/shard_map/block_0/all_to_all | solution.py:165
  86.3 12.8 %all-to-all-done.3 = f32[256,1,128]{2,1,0:T(1,128)S(1)} async-done(((f32[256,1,128]{2,1,0:T(1,128)}), f32[256,1,128]{2,1,0:T(1,128)S(1)}, u32[]{:S(2)}, u32[]{:S(2)}) %all-to-all-start.3) | async-done | bytes 131104 | tf_op jit(solution)/shard_map/block_0/all_to_all | solution.py:165
  100.7 5.7 %all-to-all-start.4 = ((f32[256,4,128]{2,1,0:T(4,128)}), f32[256,4,128]{2,1,0:T(4,128)S(1)}, u32[]{:S(2)}, u32[]{:S(2)}) async-start(f32[256,4,128]{2,1,0:T(4,128)} %broadcast_in_dim.138), calls=%async_computation.4 | async-start | bytes 1048576 | tf_op jit(solution)/shard_map/block_0/all_to_all | solution.py:165
  106.4 20.0 %all-to-all-done.4 = f32[256,4,128]{2,1,0:T(4,128)S(1)} async-done(((f32[256,4,128]{2,1,0:T(4,128)}), f32[256,4,128]{2,1,0:T(4,128)S(1)}, u32[]{:S(2)}, u32[]{:S(2)}) %all-to-all-start.4) | async-done | bytes 524320 | tf_op jit(solution)/shard_map/block_0/all_to_all | solution.py:165
  127.3 19.0 %all_to_all.70 = f32[256,1,128]{2,1,0:T(1,128)S(1)} all-to-all(f32[256,1,128]{2,1,0:T(1,128)S(1)} %broadcast_in_dim.140), channel_id=1, replica_groups=mesh['z'=8,'y'=4,'xh'=2,'sy'=2,'sx'=2] {'z','y','xh','sy','sx'}, dimensions={0} | all-to-all | bytes 262144 | tf_op jit(solution)/shard_map/block_1/all_to_all | solution.py:165
  146.3 1.8 block_1.3
  148.8 5.5 %all-to-all-start.6 = ((f32[256,1,128]{2,1,0:T(1,128)}), f32[256,1,128]{2,1,0:T(1,128)S(1)}, u32[]{:S(2)}, u32[]{:S(2)}) async-start(f32[256,1,128]{2,1,0:T(1,128)} %broadcast_in_dim.142), calls=%async_computation.6 | async-start | bytes 262144 | tf_op jit(solution)/shard_map/block_1/all_to_all | solution.py:165
  154.4 13.0 %all-to-all-done.6 = f32[256,1,128]{2,1,0:T(1,128)S(1)} async-done(((f32[256,1,128]{2,1,0:T(1,128)}), f32[256,1,128]{2,1,0:T(1,128)S(1)}, u32[]{:S(2)}, u32[]{:S(2)}) %all-to-all-start.6) | async-done | bytes 131104 | tf_op jit(solution)/shard_map/block_1/all_to_all | solution.py:165
  168.2 25.3 %all_to_all.71 = f32[256,4,128]{2,1,0:T(4,128)S(1)} all-to-all(f32[256,4,128]{2,1,0:T(4,128)S(1)} %broadcast_in_dim.144), channel_id=1, replica_groups=mesh['z'=8,'y'=4,'xh'=2,'sy'=2,'sx'=2] {'z','y','xh','sy','sx'}, dimensions={0} | all-to-all | bytes 1048576 | tf_op jit(solution)/shard_map/block_1/all_to_all | solution.py:165
  194.3 19.0 %all_to_all.72 = f32[256,1,128]{2,1,0:T(1,128)S(1)} all-to-all(f32[256,1,128]{2,1,0:T(1,128)S(1)} %broadcast_in_dim.146), channel_id=1, replica_groups=mesh['z'=8,'y'=4,'xh'=2,'sy'=2,'sx'=2] {'z','y','xh','sy','sx'}, dimensions={0} | all-to-all | bytes 262144 | tf_op jit(solution)/shard_map/block_2/all_to_all | solution.py:165
  213.3 1.8 block_2.3
  215.8 5.7 %all-to-all-start.9 = ((f32[256,1,128]{2,1,0:T(1,128)}), f32[256,1,128]{2,1,0:T(1,128)S(1)}, u32[]{:S(2)}, u32[]{:S(2)}) async-start(f32[256,1,128]{2,1,0:T(1,128)} %broadcast_in_dim.148), calls=%async_computation.9 | async-start | bytes 262144 | tf_op jit(solution)/shard_map/block_2/all_to_all | solution.py:165
  221.6 12.9 %all-to-all-done.9 = f32[256,1,128]{2,1,0:T(1,128)S(1)} async-done(((f32[256,1,128]{2,1,0:T(1,128)}), f32[256,1,128]{2,1,0:T(1,128)S(1)}, u32[]{:S(2)}, u32[]{:S(2)}) %all-to-all-start.9) | async-done | bytes 131104 | tf_op jit(solution)/shard_map/block_2/all_to_all | solution.py:165
  235.4 4.6 %all-to-all-start.12 = ((f32[64,24,128]{2,1,0:T(8,128)}), f32[64,24,128]{2,1,0:T(8,128)S(1)}, u32[]{:S(2)}, u32[]{:S(2)}) async-start(f32[64,24,128]{2,1,0:T(8,128)} %broadcast_in_dim.157), calls=%async_computation.12 | async-start | bytes 1572864 | tf_op jit(solution)/shard_map/class/all_to_all | solution.py:165
  240.9 21.3 %all-to-all-done.12 = f32[64,24,128]{2,1,0:T(8,128)S(1)} async-done(((f32[64,24,128]{2,1,0:T(8,128)}), f32[64,24,128]{2,1,0:T(8,128)S(1)}, u32[]{:S(2)}, u32[]{:S(2)}) %all-to-all-start.12) | async-done | bytes 786464 | tf_op jit(solution)/shard_map/class/all_to_all | solution.py:165
  263.1 9.2 %all-to-all-start.10 = ((f32[256,4,128]{2,1,0:T(4,128)}), f32[256,4,128]{2,1,0:T(4,128)S(1)}, u32[]{:S(2)}, u32[]{:S(2)}) async-start(f32[256,4,128]{2,1,0:T(4,128)} %broadcast_in_dim.150), calls=%async_computation.10 | async-start | bytes 1048576 | tf_op jit(solution)/shard_map/block_2/all_to_all | solution.py:165
  273.1 1.2 fusion.19
  274.4 17.8 %all-to-all-done.10 = f32[256,4,128]{2,1,0:T(4,128)S(1)} async-done(((f32[256,4,128]{2,1,0:T(4,128)}), f32[256,4,128]{2,1,0:T(4,128)S(1)}, u32[]{:S(2)}, u32[]{:S(2)}) %all-to-all-start.10) | async-done | bytes 524320 | tf_op jit(solution)/shard_map/block_2/all_to_all | solution.py:165
  293.2 5.9 %all-to-all-start.13 = ((bf16[64,32,128]{2,1,0:T(8,128)(2,1)}), bf16[64,32,128]{2,1,0:T(8,128)(2,1)S(1)}, u32[]{:S(2)}, u32[]{:S(2)}) async-start(bf16[64,32,128]{2,1,0:T(8,128)(2,1)} %broadcast_in_dim.159), calls=%async_computation.13 | async-start | bytes 1048576 | tf_op jit(solution)/shard_map/class/all_to_all | solution.py:165
  301.9 14.4 %all-to-all-done.13 = bf16[64,32,128]{2,1,0:T(8,128)(2,1)S(1)} async-done(((bf16[64,32,128]{2,1,0:T(8,128)(2,1)}), bf16[64,32,128]{2,1,0:T(8,128)(2,1)S(1)}, u32[]{:S(2)}, u32[]{:S(2)}) %all-to-all-start.13) | async-done | bytes 524320 | tf_op jit(solution)/shard_map/class/all_to_all | solution.py:165
  317.2 8.4 %all-to-all-start.11 = ((f32[256,4,128]{2,1,0:T(4,128)}), f32[256,4,128]{2,1,0:T(4,128)S(1)}, u32[]{:S(2)}, u32[]{:S(2)}) async-start(f32[256,4,128]{2,1,0:T(4,128)} %broadcast_in_dim.155), calls=%async_computation.11 | async-start | bytes 1048576 | tf_op jit(solution)/shard_map/loss/all_to_all | solution.py:165
  325.9 19.6 %all-to-all-done.11 = f32[256,4,128]{2,1,0:T(4,128)S(1)} async-done(((f32[256,4,128]{2,1,0:T(4,128)}), f32[256,4,128]{2,1,0:T(4,128)S(1)}, u32[]{:S(2)}, u32[]{:S(2)}) %all-to-all-start.11) | async-done | bytes 524320 | tf_op jit(solution)/shard_map/loss/all_to_all | solution.py:165
  345.9 1.2 fusion.2
  (123 shorter events, 29.1 us)
Async XLA Ops:
  1.5 40.3 %collective-permute-start = (bf16[4,28,256]{2,1,0:T(8,128)(2,1)S(1)}, bf16[4,28,256]{2,1,0:T(8,128)(2,1)S(1)}, u32[]{:S(2)}, u32[]{:S(2)}) collective-permute-start(bf16[4,28,256]{2,1,0:T(8,128)(2,1)S(1)} %select_bitcast_fusion), channel_id=1, source_target_pairs={{0,2},{2,0},{1,3},{3,1},{4,6},{6,4},{5,7},{7,5},{8,10},{10,8},{9,1... | collective-permute-start | bytes 172040 | tf_op jit(solution)/shard_map/halo/ppermute | solution.py:139
  3.7 38.1 %collective-permute-start.2 = (bf16[4,4,256]{2,1,0:T(4,128)(2,1)S(1)}, bf16[4,4,256]{2,1,0:T(4,128)(2,1)S(1)}, u32[]{:S(2)}, u32[]{:S(2)}) collective-permute-start(bf16[4,4,256]{2,1,0:T(4,128)(2,1)S(1)} %slice_select_fusion.1), channel_id=1, source_target_pairs={{0,3},{1,2},{2,1},{3,0},{4,7},{5,6},{6,5},{7,4},{8,11},{9,10},{10,... | collective-permute-start | bytes 24584 | tf_op jit(solution)/shard_map/halo/ppermute | solution.py:140
  6.6 1.1 copy-start.7
  7.6 0.7 copy-start.15
  7.6 34.1 %collective-permute-start.1 = (bf16[28,4,256]{2,1,0:T(4,128)(2,1)S(1)}, bf16[28,4,256]{2,1,0:T(4,128)(2,1)S(1)}, u32[]{:S(2)}, u32[]{:S(2)}) collective-permute-start(bf16[28,4,256]{2,1,0:T(4,128)(2,1)S(1)} %slice_select_fusion), channel_id=1, source_target_pairs={{0,1},{1,0},{2,3},{3,2},{4,5},{5,4},{6,7},{7,6},{8,9},{9,8},{10,11... | collective-permute-start | bytes 172040 | tf_op jit(solution)/shard_map/halo/ppermute | solution.py:138
  8.2 0.7 copy-start.9
  11.1 12.7 %copy-start.4 = (bf16[3,3,3,64,1]{3,2,4,1,0:T(4,128)(2,1)S(1)}, bf16[3,3,3,64,1]{3,2,4,1,0:T(4,128)(2,1)}, u32[]{:S(2)}) copy-start(bf16[3,3,3,64,1]{3,2,4,1,0:T(4,128)(2,1)} %param.20) | copy-start | bytes 10372
  11.1 23.4 %all-to-all-start = ((bf16[64,2,128]{2,1,0:T(2,128)(2,1)}), bf16[64,2,128]{2,1,0:T(2,128)(2,1)S(1)}, u32[]{:S(2)}, u32[]{:S(2)}) async-start(bf16[64,2,128]{2,1,0:T(2,128)(2,1)} %broadcast_in_dim.130), calls=%async_computation | async-start | bytes 65536 | tf_op jit(solution)/shard_map/filters/all_to_all | solution.py:165
  23.8 0.7 copy-start.3
  26.3 0.7 copy-start.6
  26.3 0.7 copy-start.8
  35.3 6.3 %copy-start.10 = (f32[3,2,64]{2,1,0:T(2,128)S(1)}, f32[3,2,64]{2,1,0:T(2,128)}, u32[]{:S(2)}) copy-start(f32[3,2,64]{2,1,0:T(2,128)} %param.28) | copy-start | bytes 4612
  35.3 6.3 %copy-start.11 = (f32[3,2,64]{2,1,0:T(2,128)S(1)}, f32[3,2,64]{2,1,0:T(2,128)}, u32[]{:S(2)}) copy-start(f32[3,2,64]{2,1,0:T(2,128)} %param.27) | copy-start | bytes 4612
  35.4 6.5 %copy-start.1 = (bf16[1,28,28,256]{3,2,1,0:T(8,128)(2,1)S(1)}, bf16[1,28,28,256]{3,2,1,0:T(8,128)(2,1)}, u32[]{:S(2)}) copy-start(bf16[1,28,28,256]{3,2,1,0:T(8,128)(2,1)} %param.16) | copy-start | bytes 1204228
  35.4 20.8 %all-to-all-start.2 = ((bf16[64,24,128]{2,1,0:T(8,128)(2,1)}), bf16[64,24,128]{2,1,0:T(8,128)(2,1)S(1)}, u32[]{:S(2)}, u32[]{:S(2)}) async-start(bf16[64,24,128]{2,1,0:T(8,128)(2,1)} %broadcast_in_dim.134), calls=%async_computation.2 | async-start | bytes 786432 | tf_op jit(solution)/shard_map/filters/all_to_all | solution.py:165
  56.9 21.2 %all-to-all-start.1 = ((f32[256,1,128]{2,1,0:T(1,128)}), f32[256,1,128]{2,1,0:T(1,128)S(1)}, u32[]{:S(2)}, u32[]{:S(2)}) async-start(f32[256,1,128]{2,1,0:T(1,128)} %broadcast_in_dim.132), calls=%async_computation.1 | async-start | bytes 262144 | tf_op jit(solution)/shard_map/block_0/all_to_all | solution.py:165
  80.5 18.6 %all-to-all-start.3 = ((f32[256,1,128]{2,1,0:T(1,128)}), f32[256,1,128]{2,1,0:T(1,128)S(1)}, u32[]{:S(2)}, u32[]{:S(2)}) async-start(f32[256,1,128]{2,1,0:T(1,128)} %broadcast_in_dim.136), calls=%async_computation.3 | async-start | bytes 262144 | tf_op jit(solution)/shard_map/block_0/all_to_all | solution.py:165
  100.7 5.7 %copy-start.12 = (f32[3,256]{1,0:T(4,128)S(1)}, f32[3,256]{1,0:T(4,128)}, u32[]{:S(2)}) copy-start(f32[3,256]{1,0:T(4,128)} %param.30) | copy-start | bytes 9220
  100.7 5.7 %copy-start.13 = (f32[3,256]{1,0:T(4,128)S(1)}, f32[3,256]{1,0:T(4,128)}, u32[]{:S(2)}) copy-start(f32[3,256]{1,0:T(4,128)} %param.29) | copy-start | bytes 9220
  100.7 25.7 %all-to-all-start.4 = ((f32[256,4,128]{2,1,0:T(4,128)}), f32[256,4,128]{2,1,0:T(4,128)S(1)}, u32[]{:S(2)}, u32[]{:S(2)}) async-start(f32[256,4,128]{2,1,0:T(4,128)} %broadcast_in_dim.138), calls=%async_computation.4 | async-start | bytes 1048576 | tf_op jit(solution)/shard_map/block_0/all_to_all | solution.py:165
  148.8 18.6 %all-to-all-start.6 = ((f32[256,1,128]{2,1,0:T(1,128)}), f32[256,1,128]{2,1,0:T(1,128)S(1)}, u32[]{:S(2)}, u32[]{:S(2)}) async-start(f32[256,1,128]{2,1,0:T(1,128)} %broadcast_in_dim.142), calls=%async_computation.6 | async-start | bytes 262144 | tf_op jit(solution)/shard_map/block_1/all_to_all | solution.py:165
  215.8 5.7 %copy-start.2 = (bf16[2,4,1000]{2,1,0:T(4,128)(2,1)S(1)}, bf16[2,4,1000]{2,1,0:T(4,128)(2,1)}, u32[]{:S(2)}) copy-start(bf16[2,4,1000]{2,1,0:T(4,128)(2,1)} %param.26) | copy-start | bytes 48004
  215.8 5.7 %copy-start.5 = (bf16[4,1000]{1,0:T(4,128)(2,1)S(1)}, bf16[4,1000]{1,0:T(4,128)(2,1)}, u32[]{:S(2)}) copy-start(bf16[4,1000]{1,0:T(4,128)(2,1)} %param.22) | copy-start | bytes 24004
  215.8 18.7 %all-to-all-start.9 = ((f32[256,1,128]{2,1,0:T(1,128)}), f32[256,1,128]{2,1,0:T(1,128)S(1)}, u32[]{:S(2)}, u32[]{:S(2)}) async-start(f32[256,1,128]{2,1,0:T(1,128)} %broadcast_in_dim.148), calls=%async_computation.9 | async-start | bytes 262144 | tf_op jit(solution)/shard_map/block_2/all_to_all | solution.py:165
  235.4 26.8 %all-to-all-start.12 = ((f32[64,24,128]{2,1,0:T(8,128)}), f32[64,24,128]{2,1,0:T(8,128)S(1)}, u32[]{:S(2)}, u32[]{:S(2)}) async-start(f32[64,24,128]{2,1,0:T(8,128)} %broadcast_in_dim.157), calls=%async_computation.12 | async-start | bytes 1572864 | tf_op jit(solution)/shard_map/class/all_to_all | solution.py:165
  263.1 29.1 %all-to-all-start.10 = ((f32[256,4,128]{2,1,0:T(4,128)}), f32[256,4,128]{2,1,0:T(4,128)S(1)}, u32[]{:S(2)}, u32[]{:S(2)}) async-start(f32[256,4,128]{2,1,0:T(4,128)} %broadcast_in_dim.150), calls=%async_computation.10 | async-start | bytes 1048576 | tf_op jit(solution)/shard_map/block_2/all_to_all | solution.py:165
  272.4 0.7 copy-start.14
  292.2 1.0 copy-start
  293.2 23.1 %all-to-all-start.13 = ((bf16[64,32,128]{2,1,0:T(8,128)(2,1)}), bf16[64,32,128]{2,1,0:T(8,128)(2,1)S(1)}, u32[]{:S(2)}, u32[]{:S(2)}) async-start(bf16[64,32,128]{2,1,0:T(8,128)(2,1)} %broadcast_in_dim.159), calls=%async_computation.13 | async-start | bytes 1048576 | tf_op jit(solution)/shard_map/class/all_to_all | solution.py:165
  317.2 28.3 %all-to-all-start.11 = ((f32[256,4,128]{2,1,0:T(4,128)}), f32[256,4,128]{2,1,0:T(4,128)S(1)}, u32[]{:S(2)}, u32[]{:S(2)}) async-start(f32[256,4,128]{2,1,0:T(4,128)} %broadcast_in_dim.155), calls=%async_computation.11 | async-start | bytes 1048576 | tf_op jit(solution)/shard_map/loss/all_to_all | solution.py:165
